TPU v7x, 256 devices: a whole 4x4x8 slice. The times are simulated.
256 devices in a mesh: loop: 32 (over x_hi, z, core), tensor: 8 (over y, x_lo).
Axes of the slice: x: 4 (x_hi: 2, x_lo: 2; x = x_hi * 2 + x_lo), y: 4, z: 8, core: 2. Of those that a mesh axis runs over, the one named last changes fastest.
Arguments:
- context: bfloat16 [10240, 5120], P('loop', 'tensor'), may hold values from -6 to 6
- w_out: bfloat16 [5120, 5120], P('tensor', 'loop'), may hold values from -0.078125 to 0.078125
- residual: bfloat16 [10240, 5120], P('loop', 'tensor'), may hold values from -70 to 70
- gain: float32 [5120], replicated, may hold values from 0.1 to 1.9
- grad_out: bfloat16 [10240, 5120], P('loop', 'tensor'), may hold values from -6 to 6
Outputs:
- normed: bfloat16 [10240, 5120], P('loop', 'tensor')
- d_context: bfloat16 [10240, 5120], P('loop', 'tensor')
- w_grad: float32 [5120, 5120], P('loop', 'tensor')
All inputs are finite; a program needn't handle non-finite values.
Results may differ from a plain program's by a relative error of at most 0.0049.
Values may be sent and summed in bfloat16 or wider, within the bound.
No kernel may reach another device: no remote copies, remote signals or barrier semaphores. Data moves between devices by JAX's collectives and lax.ppermute only.
A program may use at most 128 MiB of HBM per device.

v0:
```python
import math
import jax
import jax.numpy as jnp
from jax import lax
from jax.sharding import PartitionSpec as P

D = 5120


def per_device(context, w_out, residual, gain, grad_out):
    slot = lax.axis_index("tensor")
    local = residual.shape[1]
    width = D
    partial_value = jnp.dot(
        context,
        lax.all_gather(w_out, "loop", axis=1, tiled=True),
        preferred_element_type=jnp.float32,
    )
    hidden = lax.psum_scatter(
        partial_value, "tensor", scatter_dimension=1, tiled=True
    ) + residual.astype(jnp.float32)
    own_gain = lax.dynamic_slice_in_dim(gain, slot * local, local, 0)
    scaled = own_gain[None, :] * grad_out.astype(jnp.float32)
    square_sum, cross_sum = lax.psum(
        (jnp.sum(hidden * hidden, axis=1), jnp.sum(hidden * scaled, axis=1)), "tensor"
    )
    root = lax.rsqrt(square_sum / width + 1e-06)[:, None]
    dot = (cross_sum / width)[:, None]
    normed = (hidden * root * own_gain[None, :]).astype(jnp.bfloat16)
    own_grad = (root * scaled - hidden * root * root * root * dot).astype(jnp.bfloat16)
    d_hidden = lax.all_gather(own_grad, "tensor", axis=1, tiled=True)
    columns = d_hidden
    d_sum = lax.dot_general(
        columns,
        lax.all_gather(w_out, "loop", axis=1, tiled=True),
        (((1,), (1,)), ((), ())),
        preferred_element_type=jnp.float32,
    )
    d_context = d_sum.astype(jnp.bfloat16)
    factor = 1.0 / math.sqrt(context.shape[0] * lax.axis_size("loop"))
    columns = d_hidden
    w_grad = lax.psum_scatter(
        lax.dot_general(
            columns, context, (((0,), (0,)), ((), ())), preferred_element_type=jnp.float32
        )
        * factor,
        "loop",
        scatter_dimension=0,
        tiled=True,
    )
    return (normed, d_context, w_grad)


def solution(mesh):
    return jax.shard_map(
        per_device,
        mesh=mesh,
        in_specs=(
            P("loop", "tensor"),
            P("tensor", "loop"),
            P("loop", "tensor"),
            P(),
            P("loop", "tensor"),
        ),
        out_specs=(P("loop", "tensor"), P("loop", "tensor"), P("loop", "tensor")),
        check_vma=False,
    )
```

profile of v0, /device:TPU:8, one launch (start us, length us, event | category | flops | bytes accessed | tf_op | source)
XLA Modules:
  0.0 542.7 jit_solution(374131623523673046)
XLA Ops:
  7.2 0.0 copy-start
  7.2 0.0 all-gather.3.cloned.1.call-start
  7.2 0.7 all-gather.3.cloned.1.call-update
  7.9 0.0 reduce-scatter.3.cloned.1.call-start
  8.0 100.9 %all-gather.3.cloned.1.call-done = bf16[640,5120]{0,1:T(8,128)(2,1)} async-done(((bf16[640,160]{0,1:T(8,128)(2,1)}), bf16[640,5120]{0,1:T(8,128)(2,1)}) %all-gather.3.cloned.1.call-update) | async-done | bytes 6553616 | tf_op jit(solution)/shard_map/all_gather | solution.py:16
  108.8 0.0 copy-done
  108.8 9.2 %fusion = f32[320,5120]{1,0:T(8,128)} fusion(bf16[320,640]{1,0:T(8,128)(2,1)S(1)} %copy-done, bf16[640,5120]{0,1:T(8,128)(2,1)} %all-gather.3.cloned.1.call-done), kind=kOutput, calls=%fused_computation.10 | convolution fusion | flops 2097152000 | bytes 13516800 | tf_op jit(solution)/shard_map/dot_general | solution.py:14
  118.0 0.0 copy-start.1
  118.0 0.0 copy-start.2
  118.0 0.0 reduce-scatter.3.cloned.1.call-update
  118.1 0.0 all-gather.5.cloned.1.call-start
  118.1 0.8 dynamic_slice.3
  119.0 133.1 %reduce-scatter.3.cloned.1.call-done = f32[320,640]{1,0:T(8,128)} async-done(((f32[320,5120]{1,0:T(8,128)}), f32[320,640]{1,0:T(8,128)}) %reduce-scatter.3.cloned.1.call-update) | async-done | bytes 819216 | tf_op jit(solution)/shard_map/reduce_scatter | solution.py:19
  252.0 0.0 copy-done.1
  252.0 0.0 copy-done.2
  252.0 1.4 multiply_reduce_fusion
  253.5 16.3 %all-reduce = (f32[320]{0:T(512)S(1)}, f32[320]{0:T(512)S(1)}) all-reduce(f32[320]{0:T(512)S(1)} %get-tuple-element.4, f32[320]{0:T(512)S(1)} %get-tuple-element.3), channel_id=1, replica_groups=mesh['loop'=32,'tensor'=8] {'tensor'}, use_global_device_ids=true, to_apply=%region_2.0 | all-reduce | flops 640 | bytes 5120 | tf_op jit(solution)/shard_map/psum | solution.py:24
  269.8 2.4 subtract_convert_fusion
  272.2 0.0 all-gather.5.cloned.1.call-update
  272.2 0.0 reduce-scatter.5.cloned.1.call-start
  272.2 76.4 %all-gather.5.cloned.1.call-done = bf16[320,5120]{1,0:T(8,128)(2,1)} async-done(((bf16[320,640]{1,0:T(8,128)(2,1)}), bf16[320,5120]{1,0:T(8,128)(2,1)}) %all-gather.5.cloned.1.call-update) | async-done | bytes 3276816 | tf_op jit(solution)/shard_map/all_gather | solution.py:31
  348.6 10.6 %convolution_multiply_fusion = f32[5120,640]{1,0:T(8,128)} fusion(bf16[320,5120]{1,0:T(8,128)(2,1)} %all-gather.5.cloned.1.call-done, bf16[320,640]{1,0:T(8,128)(2,1)S(1)} %copy-done), kind=kOutput, calls=%fused_computation | convolution fusion | flops 2100428800 | bytes 16793600 | tf_op jit(solution)/shard_map/dot_general | solution.py:43
  359.2 0.0 reduce-scatter.5.cloned.1.call-update
  359.2 7.3 %convolution_convert_fusion = bf16[320,640]{1,0:T(8,128)(2,1)} fusion(bf16[320,5120]{1,0:T(8,128)(2,1)} %all-gather.5.cloned.1.call-done, bf16[640,5120]{0,1:T(8,128)(2,1)} %all-gather.3.cloned.1.call-done), kind=kOutput, calls=%fused_computation.1 | convolution fusion | flops 2097356800 | bytes 10240000 | tf_op jit(solution)/shard_map/dot_general | solution.py:33
  366.5 169.6 %reduce-scatter.5.cloned.1.call-done = f32[160,640]{1,0:T(8,128)} async-done(((f32[5120,640]{1,0:T(8,128)}), f32[160,640]{1,0:T(8,128)}) %reduce-scatter.5.cloned.1.call-update) | async-done | bytes 409616 | tf_op jit(solution)/shard_map/reduce_scatter | solution.py:42
  (1 shorter events, 0.0 us)
Async XLA Ops:
  7.2 101.7 %copy-start = (bf16[320,640]{1,0:T(8,128)(2,1)S(1)}, bf16[320,640]{1,0:T(8,128)(2,1)}, u32[]{:S(2)}) copy-start(bf16[320,640]{1,0:T(8,128)(2,1)} %param.5) | copy-start | bytes 1228804
  7.2 101.6 %all-gather.3.cloned.1.call-start = ((), (), s32[]{:S(2)}) async-start(), calls=%async_computation.2 | async-start | bytes 6758400 | tf_op jit(solution)/shard_map/all_gather | solution.py:16
  7.9 244.1 %reduce-scatter.3.cloned.1.call-start = ((), (), s32[]{:S(2)}) async-start(), calls=%async_computation.3 | async-start | bytes 7372800 | tf_op jit(solution)/shard_map/reduce_scatter | solution.py:19
  118.0 134.0 %copy-start.1 = (bf16[320,640]{1,0:T(8,128)(2,1)S(1)}, bf16[320,640]{1,0:T(8,128)(2,1)}, u32[]{:S(2)}) copy-start(bf16[320,640]{1,0:T(8,128)(2,1)} %param.9) | copy-start | bytes 1228804
  118.0 134.0 %copy-start.2 = (bf16[320,640]{1,0:T(8,128)(2,1)S(1)}, bf16[320,640]{1,0:T(8,128)(2,1)}, u32[]{:S(2)}) copy-start(bf16[320,640]{1,0:T(8,128)(2,1)} %param.7) | copy-start | bytes 1228804
  118.1 230.6 %all-gather.5.cloned.1.call-start = ((), (), s32[]{:S(2)}) async-start(), calls=%async_computation.4 | async-start | bytes 3686400 | tf_op jit(solution)/shard_map/all_gather | solution.py:31
  272.2 264.0 %reduce-scatter.5.cloned.1.call-start = ((), (), s32[]{:S(2)}) async-start(), calls=%async_computation.5 | async-start | bytes 13516800 | tf_op jit(solution)/shard_map/reduce_scatter | solution.py:42
Sparse Core Ops, SparseCore 0:
  10.8 97.9 all-gather.2
  118.2 133.7 reduce-scatter.2
  272.3 76.2 all-gather.4
  359.4 176.7 reduce-scatter.4
where the time goes:
time: 543 us
  waiting for transfers between devices  481 us (89%)
  matrix products  27.1 us (5%)
  blocking collectives  16.3 us (3%)
  between operations  13.8 us (3%)
    reduce_scatter x1, waiting for transfers between devices, per_device(): lax.psum_scatter(lax.dot_general(columns, context, (((0,), (0,)), ((), ()...  170 us
    reduce_scatter x1, waiting for transfers between devices, per_device(): lax.psum_scatter(partial_value, 'tensor', scatter_dimension=1, tiled=True)  133 us
    all_gather x1, waiting for transfers between devices, per_device(): lax.all_gather(w_out, 'loop', axis=1, tiled=True)  101 us
    all_gather x1, waiting for transfers between devices, per_device(): d_hidden = lax.all_gather(own_grad, 'tensor', axis=1, tiled=True)  76.4 us
    psum x1, blocking collectives, per_device(): lax.psum((jnp.sum(hidden * hidden, axis=1), jnp.sum(hidden * scaled, axis...  16.3 us
  transfers between devices with their start and end apart: 4, of which 4 were waited for; matrix products, arithmetic and copies ran while one was open for 2% of the time, Pallas kernels for 0%

commit v1 on v0

--- a/solution.py
+++ b/solution.py
@@ -28,7 +28,9 @@
     dot = (cross_sum / width)[:, None]
     normed = (hidden * root * own_gain[None, :]).astype(jnp.bfloat16)
     own_grad = (root * scaled - hidden * root * root * root * dot).astype(jnp.bfloat16)
-    d_hidden = lax.all_gather(own_grad, "tensor", axis=1, tiled=True)
+    d_hidden = jnp.concatenate(
+        lax.all_to_all(jnp.stack([own_grad] * lax.axis_size("tensor")), "tensor", 0, 0), axis=1
+    )
     columns = d_hidden
     d_sum = lax.dot_general(
         columns,

time: 543 us -> 505 us (0.930)
  waiting for transfers between devices: 481 us -> 404 us
  blocking collectives: 16.3 us -> 55.9 us
    all_gather x1 -> x0, waiting for transfers between devices: 76.4 us -> none  [per_device(): d_hidden = lax.all_gather(own_grad, 'tensor', axis=1, tiled=True)]
    all_to_all x0 -> x1, blocking collectives: none -> 39.6 us  [per_device(): lax.all_to_all(jnp.stack([own_grad] * lax.axis_size('tensor')), 'tensor',...]
  transfers between devices with their start and end apart: 4 -> 3, of which waited for: 4 -> 3; matrix products, arithmetic and copies ran while one was open for 2% -> 2% of each run, Pallas kernels for 0% -> 0%
where the time goes in v1:
time: 505 us
  waiting for transfers between devices  404 us (80%)
  blocking collectives  55.9 us (11%)
  matrix products  23.4 us (5%)
  between operations  13.8 us (3%)
    reduce_scatter x1, waiting for transfers between devices, per_device(): lax.psum_scatter(lax.dot_general(columns, context, (((0,), (0,)), ((), ()...  170 us
    reduce_scatter x1, waiting for transfers between devices, per_device(): lax.psum_scatter(partial_value, 'tensor', scatter_dimension=1, tiled=True)  133 us
    all_gather x1, waiting for transfers between devices, per_device(): lax.all_gather(w_out, 'loop', axis=1, tiled=True)  101 us
    all_to_all x1, blocking collectives, per_device(): lax.all_to_all(jnp.stack([own_grad] * lax.axis_size('tensor')), 'tensor',...  39.6 us
    psum x1, blocking collectives, per_device(): lax.psum((jnp.sum(hidden * hidden, axis=1), jnp.sum(hidden * scaled, axis...  16.3 us
  transfers between devices with their start and end apart: 3, of which 3 were waited for; matrix products, arithmetic and copies ran while one was open for 2% of the time, Pallas kernels for 0%

profile of v1, /device:TPU:8, one launch (start us, length us, event | category | flops | bytes accessed | tf_op | source)
XLA Modules:
  0.0 504.7 jit_solution(11909428896425616147)
XLA Ops:
  7.2 0.0 copy-start
  7.2 0.0 all-gather.2.cloned.1.call-start
  7.2 0.7 all-gather.2.cloned.1.call-update
  7.9 0.0 reduce-scatter.3.cloned.1.call-start
  8.0 100.9 %all-gather.2.cloned.1.call-done = bf16[640,5120]{0,1:T(8,128)(2,1)} async-done(((bf16[640,160]{0,1:T(8,128)(2,1)}), bf16[640,5120]{0,1:T(8,128)(2,1)}) %all-gather.2.cloned.1.call-update) | async-done | bytes 6553616 | tf_op jit(solution)/shard_map/all_gather | solution.py:16
  108.8 0.0 copy-done
  108.8 9.2 %fusion = f32[320,5120]{1,0:T(8,128)} fusion(bf16[320,640]{1,0:T(8,128)(2,1)S(1)} %copy-done, bf16[640,5120]{0,1:T(8,128)(2,1)} %all-gather.2.cloned.1.call-done), kind=kOutput, calls=%fused_computation.10 | convolution fusion | flops 2097152000 | bytes 13516800 | tf_op jit(solution)/shard_map/dot_general | solution.py:14
  118.0 0.0 copy-start.2
  118.0 0.0 copy-start.3
  118.0 0.0 reduce-scatter.3.cloned.1.call-update
  118.1 0.0 reduce-scatter.5.cloned.1.call-start
  118.1 0.8 dynamic_slice.3
  118.9 133.1 %reduce-scatter.3.cloned.1.call-done = f32[320,640]{1,0:T(8,128)} async-done(((f32[320,5120]{1,0:T(8,128)}), f32[320,640]{1,0:T(8,128)}) %reduce-scatter.3.cloned.1.call-update) | async-done | bytes 819216 | tf_op jit(solution)/shard_map/reduce_scatter | solution.py:19
  252.0 0.0 copy-done.2
  252.0 0.0 copy-done.3
  252.0 1.4 multiply_reduce_fusion
  253.5 16.3 %all-reduce = (f32[320]{0:T(512)S(1)}, f32[320]{0:T(512)S(1)}) all-reduce(f32[320]{0:T(512)S(1)} %get-tuple-element.4, f32[320]{0:T(512)S(1)} %get-tuple-element.3), channel_id=1, replica_groups=mesh['loop'=32,'tensor'=8] {'tensor'}, use_global_device_ids=true, to_apply=%region_2.0 | all-reduce | flops 640 | bytes 5120 | tf_op jit(solution)/shard_map/psum | solution.py:24
  269.8 2.3 subtract_convert_fusion
  272.0 0.3 stack.2
  272.3 39.6 %all_to_all.5 = bf16[8,320,640]{2,1,0:T(8,128)(2,1)S(1)} all-to-all(bf16[8,320,640]{2,1,0:T(8,128)(2,1)S(1)} %stack.2), channel_id=1, replica_groups=mesh['loop'=32,'tensor'=8] {'tensor'}, dimensions={0} | all-to-all | bytes 6553600 | tf_op jit(solution)/shard_map/all_to_all | solution.py:32
  311.9 0.5 copy.9
  312.4 0.0 copy-start.1
  312.4 1.7 copy-done.1
  314.1 6.9 %convolution_multiply_fusion = f32[5120,640]{1,0:T(8,128)} fusion(bf16[320,5120]{1,0:T(8,128)(2,1)S(1)} %bitcast.9, bf16[320,640]{1,0:T(8,128)(2,1)S(1)} %copy-done), kind=kOutput, calls=%fused_computation | convolution fusion | flops 2100428800 | bytes 16793600 | tf_op jit(solution)/shard_map/dot_general | solution.py:45
  321.1 0.0 reduce-scatter.5.cloned.1.call-update
  321.1 7.3 %convolution_convert_fusion = bf16[320,640]{1,0:T(8,128)(2,1)} fusion(bf16[320,5120]{1,0:T(8,128)(2,1)} %bitcast.10, bf16[640,5120]{0,1:T(8,128)(2,1)} %all-gather.2.cloned.1.call-done), kind=kOutput, calls=%fused_computation.1 | convolution fusion | flops 2097356800 | bytes 10240000 | tf_op jit(solution)/shard_map/dot_general | solution.py:35
  328.4 169.8 %reduce-scatter.5.cloned.1.call-done = f32[160,640]{1,0:T(8,128)} async-done(((f32[5120,640]{1,0:T(8,128)}), f32[160,640]{1,0:T(8,128)}) %reduce-scatter.5.cloned.1.call-update) | async-done | bytes 409616 | tf_op jit(solution)/shard_map/reduce_scatter | solution.py:44
  (1 shorter events, 0.0 us)
Async XLA Ops:
  7.2 101.7 %copy-start = (bf16[320,640]{1,0:T(8,128)(2,1)S(1)}, bf16[320,640]{1,0:T(8,128)(2,1)}, u32[]{:S(2)}) copy-start(bf16[320,640]{1,0:T(8,128)(2,1)} %param.5) | copy-start | bytes 1228804
  7.2 101.6 %all-gather.2.cloned.1.call-start = ((), (), s32[]{:S(2)}) async-start(), calls=%async_computation.3 | async-start | bytes 6758400 | tf_op jit(solution)/shard_map/all_gather | solution.py:16
  7.9 244.1 %reduce-scatter.3.cloned.1.call-start = ((), (), s32[]{:S(2)}) async-start(), calls=%async_computation.4 | async-start | bytes 7372800 | tf_op jit(solution)/shard_map/reduce_scatter | solution.py:19
  118.0 134.0 %copy-start.2 = (bf16[320,640]{1,0:T(8,128)(2,1)S(1)}, bf16[320,640]{1,0:T(8,128)(2,1)}, u32[]{:S(2)}) copy-start(bf16[320,640]{1,0:T(8,128)(2,1)} %param.9) | copy-start | bytes 1228804
  118.0 134.0 %copy-start.3 = (bf16[320,640]{1,0:T(8,128)(2,1)S(1)}, bf16[320,640]{1,0:T(8,128)(2,1)}, u32[]{:S(2)}) copy-start(bf16[320,640]{1,0:T(8,128)(2,1)} %param.7) | copy-start | bytes 1228804
  118.1 380.2 %reduce-scatter.5.cloned.1.call-start = ((), (), s32[]{:S(2)}) async-start(), calls=%async_computation.5 | async-start | bytes 13516800 | tf_op jit(solution)/shard_map/reduce_scatter | solution.py:44
  312.4 1.8 copy-start.1
Sparse Core Ops, SparseCore 0:
  10.8 97.9 all-gather.1
  118.2 133.7 reduce-scatter.2
  321.2 176.9 reduce-scatter.4
